TPU v7x, 256 devices: a whole 4x4x8 slice. The times are simulated.
256 devices in a mesh: dp: 16 (over x, y), expert: 16 (over z, core).
Axes of the slice: x: 4, y: 4, z: 8, core: 2. Of those that a mesh axis runs over, the one named last changes fastest.
Arguments:
- tokens: bfloat16 [40960, 2048], P(('dp', 'expert')), may hold values from -6 to 6
- routes: int32 [40960, 2], P(('dp', 'expert')), may hold values from 0 to 15, all different within a row; in each aligned block of 160 rows (0 to 159, 160 to 319, ...) at most 30 rows name the same one
- route_gains: float32 [40960, 2], P(('dp', 'expert')), may hold values from 0.1 to 1
- cotangent: bfloat16 [40960, 2048], P(('dp', 'expert')), may hold values from -24 to 24
- w_gate: bfloat16 [16, 2048, 768], P('expert'), may hold values from -0.125 to 0.125
- w_up: bfloat16 [16, 2048, 768], P('expert'), may hold values from -0.125 to 0.125
- w_down: bfloat16 [16, 2048, 768], P('expert'), may hold values from -0.21875 to 0.21875
Outputs:
- layer_output: bfloat16 [40960, 2048], P(('dp', 'expert'))
- input_grad: bfloat16 [40960, 2048], P(('dp', 'expert'))
- grad_gate: bfloat16 [16, 2048, 768], P('expert', 'dp')
- grad_up: bfloat16 [16, 2048, 768], P('expert', 'dp')
- grad_down: bfloat16 [16, 2048, 768], P('expert', 'dp')
Inputs may be any that keep to these rules, and one draw needn't show every extreme that they name: `routes`: each row names 2 different experts. Within the rows of one device (aligned blocks of 160 rows) no expert is named more than 30 times, and in some device's rows one expert is named exactly 30 times.
All inputs are finite; a program needn't handle non-finite values.
Results may differ from a plain program's by a relative error of at most 0.015.
Values may be sent and summed in bfloat16 or wider, within the bound.
A program may use at most 128 MiB of HBM per device.

v0:
```python
import jax
import jax.numpy as jnp
from jax import lax
from jax.sharding import PartitionSpec as P

SLOTS = 32


def slot_masks(routes, experts):
    rows, picks = routes.shape
    chosen = routes.T.reshape(1, -1)
    labels = lax.broadcasted_iota(jnp.int32, (experts, rows * picks), 0)
    matches = chosen == labels
    total = rows * picks
    earlier = lax.broadcasted_iota(jnp.int32, (total, total), 0) < lax.broadcasted_iota(
        jnp.int32, (total, total), 1
    )
    before = jnp.dot(
        matches.astype(jnp.bfloat16),
        earlier.astype(jnp.bfloat16),
        preferred_element_type=jnp.float32,
    )
    position = jnp.sum(jnp.where(matches, before, 0.0), axis=0).astype(jnp.int32)
    target = chosen[0] * SLOTS + position
    slots = lax.broadcasted_iota(jnp.int32, (experts * SLOTS, total), 0)
    return (slots == target[None, :]).reshape(experts * SLOTS, picks, rows)


def rows_t(left, right):
    return lax.dot_general(
        left, right, (((1,), (1,)), ((), ())), preferred_element_type=jnp.float32
    )


def outer_rows(left, right):
    return lax.dot_general(
        left, right, (((0,), (0,)), ((), ())), preferred_element_type=jnp.float32
    )


def shards(tokens, routes, route_gains, cotangent, w_gate, w_up, w_down):
    experts = lax.axis_size("expert")
    groups = lax.axis_size("dp")
    width = tokens.shape[1]
    depth = width // groups
    flip = [(a * experts + b, b * experts + a) for a in range(groups) for b in range(experts)]
    mine = lax.axis_index("dp") * depth
    hidden_units = w_gate.shape[2]

    def fetch(w):
        part = lax.dynamic_slice_in_dim(w[0], mine, depth, axis=0)
        return part

    part = jnp.concatenate([fetch(w_gate), fetch(w_up), fetch(w_down)], axis=1)
    part = lax.ppermute(part, ("dp", "expert"), flip)
    full = lax.all_gather(part, "expert", axis=0, tiled=True)
    gate_mat = full[:, :hidden_units]
    up_mat = full[:, hidden_units : 2 * hidden_units]
    down_mat = full[:, 2 * hidden_units :]
    masks = slot_masks(routes, groups)
    first = masks[:, 0, :].astype(jnp.bfloat16)
    second = masks[:, 1, :].astype(jnp.bfloat16)
    both = first + second
    gains = route_gains.T
    slot_gain = jnp.sum(jnp.where(masks, gains[None], 0.0), axis=(1, 2))
    send_tok = jnp.dot(both, tokens, preferred_element_type=jnp.float32).astype(jnp.bfloat16)
    send_cot = (
        slot_gain[:, None] * jnp.dot(both, cotangent, preferred_element_type=jnp.float32)
    ).astype(jnp.bfloat16)

    def exchange(block):
        block = block.reshape(groups, SLOTS, width)
        block = lax.all_to_all(block, "dp", split_axis=0, concat_axis=0, tiled=True)
        return block.reshape(groups * SLOTS, width)

    arrived = exchange(send_tok)
    arrived_cot = exchange(send_cot)
    pre_gate = jnp.dot(arrived, gate_mat, preferred_element_type=jnp.float32)
    pre_up = jnp.dot(arrived, up_mat, preferred_element_type=jnp.float32)
    sigma = jax.nn.sigmoid(pre_gate)
    activated = pre_gate * sigma
    hidden = (activated * pre_up).astype(jnp.bfloat16)
    d_hidden = jnp.dot(arrived_cot, down_mat, preferred_element_type=jnp.float32)
    d_gate = (d_hidden * pre_up * (sigma * (1.0 + pre_gate * (1.0 - sigma)))).astype(jnp.bfloat16)
    d_up = (d_hidden * activated).astype(jnp.bfloat16)
    partial = jnp.concatenate(
        [outer_rows(arrived, d_gate), outer_rows(arrived, d_up), outer_rows(arrived_cot, hidden)],
        axis=1,
    ).astype(jnp.bfloat16)
    summed = lax.psum_scatter(partial, "expert", scatter_dimension=0, tiled=True)
    produced = rows_t(hidden, down_mat).astype(jnp.bfloat16)
    d_pick = (rows_t(d_gate, gate_mat) + rows_t(d_up, up_mat)).astype(jnp.bfloat16)
    back_out = exchange(produced)
    back_grad = exchange(d_pick)
    layer_output = (
        gains[0][:, None] * outer_rows(first, back_out)
        + gains[1][:, None] * outer_rows(second, back_out)
    ).astype(jnp.bfloat16)
    input_grad = (outer_rows(first, back_grad) + outer_rows(second, back_grad)).astype(jnp.bfloat16)
    summed = lax.ppermute(summed, ("dp", "expert"), flip)
    grad_gate = summed[None, :, :hidden_units]
    grad_up = summed[None, :, hidden_units : 2 * hidden_units]
    grad_down = summed[None, :, 2 * hidden_units :]
    return (layer_output, input_grad, grad_gate, grad_up, grad_down)


def solution(mesh):
    rows = P(("dp", "expert"), None)
    weights = P("expert", None, None)
    shares = P("expert", "dp", None)
    return jax.shard_map(
        shards,
        mesh=mesh,
        in_specs=(rows, rows, rows, rows, weights, weights, weights),
        out_specs=(rows, rows, shares, shares, shares),
        check_vma=False,
    )
```

profile of v0, /device:TPU:14, one launch (start us, length us, event | category | flops | bytes accessed | tf_op | source)
XLA Modules:
  0.0 330.9 jit_solution(815282746643636325)
XLA Ops:
  7.2 0.0 copy-start
  7.2 0.0 copy-start.10
  7.2 0.0 copy-start.9
  7.2 0.0 all-gather.2.cloned.1.call-start
  7.3 1.8 copy-done
  9.1 0.0 copy-start.11
  9.1 1.1 dynamic-slice_bitcast_fusion
  10.3 7.4 %collective-permute-start = (bf16[128,2304]{1,0:T(8,128)(2,1)S(1)}, bf16[128,2304]{1,0:T(8,128)(2,1)S(1)}, u32[]{:S(2)}, u32[]{:S(2)}) collective-permute-start(bf16[128,2304]{1,0:T(8,128)(2,1)S(1)} %pad_maximum_fusion.1), channel_id=1, source_target_pairs={{0,0},{1,16},{2,32},{3,48},{4,64},{5,80},{6,96},{7,112},{8,128},{9... | collective-permute-start | bytes 1769480 | tf_op jit(solution)/shard_map/ppermute | solution.py:55
  17.7 56.6 %collective-permute-done = bf16[128,2304]{1,0:T(8,128)(2,1)S(1)} collective-permute-done((bf16[128,2304]{1,0:T(8,128)(2,1)S(1)}, bf16[128,2304]{1,0:T(8,128)(2,1)S(1)}, u32[]{:S(2)}, u32[]{:S(2)}) %collective-permute-start) | collective-permute-done | bytes 589856 | tf_op jit(solution)/shard_map/ppermute | solution.py:55
  74.3 0.8 copy-done.8
  75.2 0.0 all-gather.2.cloned.1.call-update
  75.2 0.1 broadcast_in_dim.31
  75.3 0.1 eq.24
  75.4 0.2 fusion.14
  75.6 0.1 convert_element_type.48
  75.6 0.2 select_reduce_fusion
  75.8 0.2 iota_compare_fusion.1
  76.0 2.1 multiply_convert_fusion
  78.1 5.6 %all-to-all-start.2 = ((bf16[16,32,2048]{2,1,0:T(8,128)(2,1)}), bf16[16,32,2048]{2,1,0:T(8,128)(2,1)S(1)}, u32[]{:S(2)}, u32[]{:S(2)}) async-start(bf16[16,32,2048]{2,1,0:T(8,128)(2,1)} %bitcast.72), calls=%async_computation.2 | async-start | bytes 4194304 | tf_op jit(solution)/shard_map/all_to_all | solution.py:73
  83.7 2.1 convolution_convert_fusion.3
  85.8 23.9 %all-to-all-done.2 = bf16[16,32,2048]{2,1,0:T(8,128)(2,1)S(1)} async-done(((bf16[16,32,2048]{2,1,0:T(8,128)(2,1)}), bf16[16,32,2048]{2,1,0:T(8,128)(2,1)S(1)}, u32[]{:S(2)}, u32[]{:S(2)}) %all-to-all-start.2) | async-done | bytes 2097184 | tf_op jit(solution)/shard_map/all_to_all | solution.py:73
  109.6 7.3 %all-to-all-start = ((bf16[16,32,2048]{2,1,0:T(8,128)(2,1)}), bf16[16,32,2048]{2,1,0:T(8,128)(2,1)}, u32[]{:S(2)}, u32[]{:S(2)}) async-start(bf16[16,32,2048]{2,1,0:T(8,128)(2,1)} %bitcast.5), calls=%async_computation | async-start | bytes 4194304 | tf_op jit(solution)/shard_map/all_to_all | solution.py:73
  117.0 0.2 reduce-scatter.4.cloned.1.call-start
  117.2 18.1 %all-gather.2.cloned.1.call-done = bf16[2048,2304]{1,0:T(8,128)(2,1)} async-done(((bf16[128,2304]{1,0:T(8,128)(2,1)}), bf16[2048,2304]{1,0:T(8,128)(2,1)}) %all-gather.2.cloned.1.call-update) | async-done | bytes 9437200 | tf_op jit(solution)/shard_map/all_gather | solution.py:56
  135.3 4.8 %fusion = f32[512,768]{1,0:T(8,128)} fusion(bf16[512,2048]{1,0:T(8,128)(2,1)S(1)} %bitcast.68, bf16[2048,2304]{1,0:T(8,128)(2,1)} %all-gather.2.cloned.1.call-done), kind=kOutput, calls=%fused_computation.8 | convolution fusion | flops 1610612736 | bytes 6815744 | tf_op jit(solution)/shard_map/dot_general | solution.py:83
  140.1 0.1 all-to-all-done
  140.2 4.4 %fusion.5 = f32[512,768]{1,0:T(8,128)S(1)} fusion(bf16[512,2048]{1,0:T(8,128)(2,1)} %bitcast.6, bf16[2048,2304]{1,0:T(8,128)(2,1)} %all-gather.2.cloned.1.call-done), kind=kOutput, calls=%fused_computation.13 | convolution fusion | flops 1610612736 | bytes 6815744 | tf_op jit(solution)/shard_map/dot_general | solution.py:79
  144.7 5.0 %multiply_convert_fusion.2 = (bf16[512,768]{1,0:T(8,128)(2,1)S(1)}, bf16[512,768]{1,0:T(8,128)(2,1)S(1)}, bf16[512,768]{1,0:T(8,128)(2,1)S(1)}) fusion(f32[512,768]{1,0:T(8,128)S(1)} %copy-done.16, f32[512,768]{1,0:T(8,128)S(1)} %fusion.5, bf16[512,2048]{1,0:T(8,128)(2,1)} %bitcast.6, bf16[2048,2304]{1,0:T(8,128)(2,1)} %all-gather.2.cloned.1.call-done), kind=kOutput, calls=%fused_computation.25 | convolution fusion | flops 1616510976 | bytes 10747904 | tf_op jit(solution)/shard_map/dot_general | solution.py:78
  149.7 0.0 copy-start.17
  149.7 0.0 copy-start.14
  149.7 0.0 copy-start.12
  149.7 0.0 copy-done.6
  149.7 1.8 convolution_convert_fusion
  151.6 3.4 %convolution_convert_fusion.1 = bf16[2048,768]{0,1:T(8,128)(2,1)S(1)} fusion(bf16[512,2048]{1,0:T(8,128)(2,1)} %bitcast.6, bf16[512,768]{1,0:T(8,128)(2,1)S(1)} %get-tuple-element.26), kind=kOutput, calls=%fused_computation.4 | convolution fusion | flops 1612185600 | bytes 6029312 | tf_op jit(solution)/shard_map/dot_general | solution.py:36
  155.0 3.4 %convolution_convert_fusion.2 = bf16[2048,768]{0,1:T(8,128)(2,1)S(1)} fusion(bf16[512,2048]{1,0:T(8,128)(2,1)} %bitcast.6, bf16[512,768]{1,0:T(8,128)(2,1)S(1)} %get-tuple-element.25), kind=kOutput, calls=%fused_computation.5 | convolution fusion | flops 1612185600 | bytes 6029312 | tf_op jit(solution)/shard_map/dot_general | solution.py:36
  158.5 4.7 %pad_maximum_fusion = bf16[2048,2304]{0,1:T(8,128)(2,1)} fusion(bf16[2048,768]{0,1:T(8,128)(2,1)S(1)} %convolution_convert_fusion, bf16[2048,768]{0,1:T(8,128)(2,1)S(1)} %convolution_convert_fusion.1, bf16[2048,768]{0,1:T(8,128)(2,1)S(1)} %convolution_convert_fusion.2), kind=kLoop, calls=%fused_computation | loop fusion | flops 28311552 | bytes 18874368 | tf_op jit(solution)/shard_map/concatenate | solution.py:86
  163.1 12.4 %copy.25 = bf16[2048,2304]{1,0:T(8,128)(2,1)} copy(bf16[2048,2304]{0,1:T(8,128)(2,1)} %pad_maximum_fusion) | data formatting | bytes 18874368
  175.5 0.0 reduce-scatter.4.cloned.1.call-update
  175.5 1.1 copy-done.15
  176.6 3.8 %fusion.3 = f32[512,2048]{1,0:T(8,128)S(1)} fusion(bf16[512,768]{1,0:T(8,128)(2,1)S(1)} %copy-done.15, bf16[2048,2304]{1,0:T(8,128)(2,1)} %all-gather.2.cloned.1.call-done), kind=kOutput, calls=%fused_computation.11 | convolution fusion | flops 1610612736 | bytes 8126464 | tf_op jit(solution)/shard_map/dot_general | solution.py:30
  180.4 0.0 copy-done.13
  180.4 5.1 %add_convert_fusion = bf16[512,2048]{1,0:T(8,128)(2,1)} fusion(f32[512,2048]{1,0:T(8,128)S(1)} %fusion.3, bf16[512,768]{1,0:T(8,128)(2,1)S(1)} %copy-done.13, bf16[2048,2304]{1,0:T(8,128)(2,1)} %all-gather.2.cloned.1.call-done), kind=kOutput, calls=%fused_computation.1 | convolution fusion | flops 1612709888 | bytes 10223616 | tf_op jit(solution)/shard_map/dot_general | solution.py:30
  185.5 8.2 %all-to-all-start.3 = ((bf16[16,32,2048]{2,1,0:T(8,128)(2,1)}), bf16[16,32,2048]{2,1,0:T(8,128)(2,1)S(1)}, u32[]{:S(2)}, u32[]{:S(2)}) async-start(bf16[16,32,2048]{2,1,0:T(8,128)(2,1)} %bitcast.71), calls=%async_computation.3 | async-start | bytes 4194304 | tf_op jit(solution)/shard_map/all_to_all | solution.py:73
  193.8 0.0 copy-done.18
  193.8 5.0 %convolution_convert_fusion.4 = bf16[512,2048]{1,0:T(8,128)(2,1)} fusion(bf16[512,768]{1,0:T(8,128)(2,1)S(1)} %copy-done.18, bf16[2048,2304]{1,0:T(8,128)(2,1)} %all-gather.2.cloned.1.call-done), kind=kOutput, calls=%fused_computation.7 | convolution fusion | flops 1611661312 | bytes 6029312 | tf_op jit(solution)/shard_map/dot_general | solution.py:30
  198.8 21.2 %all-to-all-done.3 = bf16[16,32,2048]{2,1,0:T(8,128)(2,1)S(1)} async-done(((bf16[16,32,2048]{2,1,0:T(8,128)(2,1)}), bf16[16,32,2048]{2,1,0:T(8,128)(2,1)S(1)}, u32[]{:S(2)}, u32[]{:S(2)}) %all-to-all-start.3) | async-done | bytes 2097184 | tf_op jit(solution)/shard_map/all_to_all | solution.py:73
  220.0 1.4 copy-done.3
  221.3 7.0 %all-to-all-start.1 = ((bf16[16,32,2048]{2,1,0:T(8,128)(2,1)}), bf16[16,32,2048]{2,1,0:T(8,128)(2,1)S(1)}, u32[]{:S(2)}, u32[]{:S(2)}) async-start(bf16[16,32,2048]{2,1,0:T(8,128)(2,1)} %bitcast.70), calls=%async_computation.1 | async-start | bytes 4194304 | tf_op jit(solution)/shard_map/all_to_all | solution.py:73
  228.4 2.3 fusion.15
  230.7 0.0 copy-done.4
  230.7 1.4 fusion.11
  232.1 20.1 %reduce-scatter.4.cloned.1.call-done = bf16[128,2304]{1,0:T(8,128)(2,1)} async-done(((bf16[2048,2304]{1,0:T(8,128)(2,1)}), bf16[128,2304]{1,0:T(8,128)(2,1)}) %reduce-scatter.4.cloned.1.call-update) | async-done | bytes 589840
  252.2 2.1 copy.26
  254.4 1.9 collective-permute-start.1
  256.3 0.0 all-to-all-done.1
  256.3 1.3 copy-done.2
  257.6 0.5 convolution_multiply_fusion
  258.2 0.0 copy-start.1
  258.2 3.2 fusion.12
  261.3 57.5 %collective-permute-done.1 = bf16[128,2304]{0,1:T(8,128)(2,1)} collective-permute-done((bf16[128,2304]{0,1:T(8,128)(2,1)}, bf16[128,2304]{0,1:T(8,128)(2,1)}, u32[]{:S(2)}, u32[]{:S(2)}) %collective-permute-start.1) | collective-permute-done | bytes 589856 | tf_op jit(solution)/shard_map/ppermute | solution.py:100
  318.8 1.8 slice_bitcast_fusion.2
  320.6 1.7 copy.22
  322.4 0.8 copy.23
  323.2 0.8 copy.24
  (27 shorter events, 0.1 us)
Async XLA Ops:
  7.2 1.9 copy-start
  7.2 68.0 %copy-start.10 = (f32[160,2]{0,1:T(2,128)S(1)}, f32[160,2]{0,1:T(2,128)}, u32[]{:S(2)}) copy-start(f32[160,2]{0,1:T(2,128)} %param.9) | copy-start | bytes 3844
  7.2 68.1 %copy-start.9 = (s32[160,2]{0,1:T(2,128)S(1)}, s32[160,2]{0,1:T(2,128)}, u32[]{:S(2)}) copy-start(s32[160,2]{0,1:T(2,128)} %param.8) | copy-start | bytes 3844
  7.2 128.1 %all-gather.2.cloned.1.call-start = ((), (), s32[]{:S(2)}) async-start(), calls=%async_computation.5 | async-start | bytes 10027008 | tf_op jit(solution)/shard_map/all_gather | solution.py:56
  9.1 66.9 %copy-start.11 = (bf16[160,2048]{1,0:T(8,128)(2,1)S(1)}, bf16[160,2048]{1,0:T(8,128)(2,1)}, u32[]{:S(2)}) copy-start(bf16[160,2048]{1,0:T(8,128)(2,1)} %param.10) | copy-start | bytes 1966084
  10.3 64.1 %collective-permute-start = (bf16[128,2304]{1,0:T(8,128)(2,1)S(1)}, bf16[128,2304]{1,0:T(8,128)(2,1)S(1)}, u32[]{:S(2)}, u32[]{:S(2)}) collective-permute-start(bf16[128,2304]{1,0:T(8,128)(2,1)S(1)} %pad_maximum_fusion.1), channel_id=1, source_target_pairs={{0,0},{1,16},{2,32},{3,48},{4,64},{5,80},{6,96},{7,112},{8,128},{9... | collective-permute-start | bytes 1769480 | tf_op jit(solution)/shard_map/ppermute | solution.py:55
  74.3 0.8 copy-start.8
  78.1 5.6 %copy-start.7 = (bf16[160,2048]{1,0:T(8,128)(2,1)S(1)}, bf16[160,2048]{1,0:T(8,128)(2,1)}, u32[]{:S(2)}) copy-start(bf16[160,2048]{1,0:T(8,128)(2,1)} %param.7) | copy-start | bytes 1966084
  78.1 31.5 %all-to-all-start.2 = ((bf16[16,32,2048]{2,1,0:T(8,128)(2,1)}), bf16[16,32,2048]{2,1,0:T(8,128)(2,1)S(1)}, u32[]{:S(2)}, u32[]{:S(2)}) async-start(bf16[16,32,2048]{2,1,0:T(8,128)(2,1)} %bitcast.72), calls=%async_computation.2 | async-start | bytes 4194304 | tf_op jit(solution)/shard_map/all_to_all | solution.py:73
  109.6 25.7 %copy-start.5 = (bf16[16,32,2048]{2,1,0:T(8,128)(2,1)}, bf16[16,32,2048]{2,1,0:T(8,128)(2,1)S(1)}, u32[]{:S(2)}) copy-start(bf16[16,32,2048]{2,1,0:T(8,128)(2,1)S(1)} %all-to-all-done.2) | copy-start | bytes 6291460
  109.6 30.6 %all-to-all-start = ((bf16[16,32,2048]{2,1,0:T(8,128)(2,1)}), bf16[16,32,2048]{2,1,0:T(8,128)(2,1)}, u32[]{:S(2)}, u32[]{:S(2)}) async-start(bf16[16,32,2048]{2,1,0:T(8,128)(2,1)} %bitcast.5), calls=%async_computation | async-start | bytes 4194304 | tf_op jit(solution)/shard_map/all_to_all | solution.py:73
  117.0 135.2 %reduce-scatter.4.cloned.1.call-start = ((), (), s32[]{:S(2)}) async-start(), calls=%async_computation.6 | async-start | bytes 10027008
  140.2 4.4 %copy-start.16 = (f32[512,768]{1,0:T(8,128)S(1)}, f32[512,768]{1,0:T(8,128)}, u32[]{:S(2)}) copy-start(f32[512,768]{1,0:T(8,128)} %fusion) | copy-start | bytes 4718596
  144.7 5.0 %copy-start.6 = (bf16[16,32,2048]{2,1,0:T(8,128)(2,1)S(1)}, bf16[16,32,2048]{2,1,0:T(8,128)(2,1)}, u32[]{:S(2)}) copy-start(bf16[16,32,2048]{2,1,0:T(8,128)(2,1)} %copy-done.5) | copy-start | bytes 6291460
  149.7 1.9 copy-start.17
  149.7 1.9 copy-start.14
  149.7 5.3 %copy-start.12 = (bf16[512,768]{1,0:T(8,128)(2,1)}, bf16[512,768]{1,0:T(8,128)(2,1)S(1)}, u32[]{:S(2)}) copy-start(bf16[512,768]{1,0:T(8,128)(2,1)S(1)} %get-tuple-element.25) | copy-start | bytes 2359300
  175.5 1.1 copy-start.15
  176.6 3.8 %copy-start.13 = (bf16[512,768]{1,0:T(8,128)(2,1)S(1)}, bf16[512,768]{1,0:T(8,128)(2,1)}, u32[]{:S(2)}) copy-start(bf16[512,768]{1,0:T(8,128)(2,1)} %copy-done.12) | copy-start | bytes 2359300
  185.5 8.3 %copy-start.18 = (bf16[512,768]{1,0:T(8,128)(2,1)S(1)}, bf16[512,768]{1,0:T(8,128)(2,1)}, u32[]{:S(2)}) copy-start(bf16[512,768]{1,0:T(8,128)(2,1)} %copy-done.17) | copy-start | bytes 2359300
  185.5 34.5 %all-to-all-start.3 = ((bf16[16,32,2048]{2,1,0:T(8,128)(2,1)}), bf16[16,32,2048]{2,1,0:T(8,128)(2,1)S(1)}, u32[]{:S(2)}, u32[]{:S(2)}) async-start(bf16[16,32,2048]{2,1,0:T(8,128)(2,1)} %bitcast.71), calls=%async_computation.3 | async-start | bytes 4194304 | tf_op jit(solution)/shard_map/all_to_all | solution.py:73
  220.0 1.4 copy-start.3
  221.3 34.9 %all-to-all-start.1 = ((bf16[16,32,2048]{2,1,0:T(8,128)(2,1)}), bf16[16,32,2048]{2,1,0:T(8,128)(2,1)S(1)}, u32[]{:S(2)}, u32[]{:S(2)}) async-start(bf16[16,32,2048]{2,1,0:T(8,128)(2,1)} %bitcast.70), calls=%async_computation.1 | async-start | bytes 4194304 | tf_op jit(solution)/shard_map/all_to_all | solution.py:73
  228.4 2.4 copy-start.4
  254.4 64.5 %collective-permute-start.1 = (bf16[128,2304]{0,1:T(8,128)(2,1)}, bf16[128,2304]{0,1:T(8,128)(2,1)}, u32[]{:S(2)}, u32[]{:S(2)}) collective-permute-start(bf16[128,2304]{0,1:T(8,128)(2,1)} %copy.26), channel_id=1, source_target_pairs={{0,0},{1,16},{2,32},{3,48},{4,64},{5,80},{6,96},{7,112},{8,128},{9... | collective-permute-start | bytes 1769480 | tf_op jit(solution)/shard_map/ppermute | solution.py:100
  256.3 1.4 copy-start.2
  258.2 65.9 %copy-start.1 = (bf16[1,2048,768]{2,1,0:T(8,128)(2,1)S(1)}, bf16[1,2048,768]{2,1,0:T(8,128)(2,1)}, u32[]{:S(2)}) copy-start(bf16[1,2048,768]{2,1,0:T(8,128)(2,1)} %param.11) | copy-start | bytes 9437188
Sparse Core Ops, SparseCore 0:
  75.3 59.9 all-gather.1
  175.6 76.5 reduce-scatter.3
where the time goes:
time: 332 us; the launch traced here: 331 us
  waiting for transfers between devices  198 us (60%)
  matrix products  48.6 us (15%)
  starting transfers between devices  37.8 us (11%)
  local copies, waits for them, and re-layouts  27.6 us (8%)
  between operations  14.3 us (4%)
  other arithmetic  5.04 us (2%)
    ppermute x1, waiting for transfers between devices, shards(): summed = lax.ppermute(summed, ('dp', 'expert'), flip)  57.5 us
    ppermute x1, waiting for transfers between devices, shards(): part = lax.ppermute(part, ('dp', 'expert'), flip)  56.6 us
    all_to_all x4, waiting for transfers between devices, exchange(): block = lax.all_to_all(block, 'dp', split_axis=0, concat_axis=0, tiled=True)  45.1 us
    all_to_all x4, starting transfers between devices, exchange(): block = lax.all_to_all(block, 'dp', split_axis=0, concat_axis=0, tiled=True)  28.2 us
    unnamed x43, local copies, waits for them, and re-layouts  24.4 us
    unnamed x3, waiting for transfers between devices  20.2 us
    all_gather x1, waiting for transfers between devices, shards(): full = lax.all_gather(part, 'expert', axis=0, tiled=True)  18.1 us
    dot_general x7, matrix products, outer_rows(): lax.dot_general(left, right, (((0,), (0,)), ((), ())), preferred_element_...  16.1 us
  transfers between devices with their start and end apart: 8, of which 7 were waited for; matrix products, arithmetic and copies ran while one was open for 10% of the time, Pallas kernels for 0%

commit v1 on v0

--- a/solution.py
+++ b/solution.py
@@ -53,7 +53,15 @@
 
     part = jnp.concatenate([fetch(w_gate), fetch(w_up), fetch(w_down)], axis=1)
     part = lax.ppermute(part, ("dp", "expert"), flip)
-    full = lax.all_gather(part, "expert", axis=0, tiled=True)
+    full = jnp.concatenate(
+        lax.all_to_all(
+            jnp.stack(lax.psum(1, axis_name="expert") * [part], axis=0),
+            axis_name="expert",
+            split_axis=0,
+            concat_axis=0,
+        ),
+        axis=0,
+    )
     gate_mat = full[:, :hidden_units]
     up_mat = full[:, hidden_units : 2 * hidden_units]
     down_mat = full[:, 2 * hidden_units :]

time: 332 us -> 536 us (1.61)
  waiting for transfers between devices: 198 us -> 378 us
  starting transfers between devices: 37.8 us -> 56.4 us
    all_to_all x0 -> x1, waiting for transfers between devices: none -> 205 us  [shards(): lax.all_to_all(jnp.stack(lax.psum(1, axis_name='expert') * [part], axis=0...]
    all_to_all x0 -> x1, starting transfers between devices: none -> 18.8 us  [shards(): lax.all_to_all(jnp.stack(lax.psum(1, axis_name='expert') * [part], axis=0...]
    all_gather x1 -> x0, waiting for transfers between devices: 18.1 us -> none  [shards(): full = lax.all_gather(part, 'expert', axis=0, tiled=True)]
    unnamed x43 -> x37, local copies, waits for them, and re-layouts: 24.4 us -> 22 us
    unnamed x3 -> x2, waiting for transfers between devices: 20.2 us -> 18.8 us
  transfers between devices with their start and end apart: 8 -> 8, of which waited for: 7 -> 6; matrix products, arithmetic and copies ran while one was open for 10% -> 6% of each run, Pallas kernels for 0% -> 0%
where the time goes in v1:
time: 536 us; the launch traced here: 535 us
  waiting for transfers between devices  378 us (71%)
  starting transfers between devices  56.4 us (11%)
  matrix products  49.3 us (9%)
  local copies, waits for them, and re-layouts  31.2 us (6%)
  between operations  14.3 us (3%)
  other arithmetic  5.73 us (1%)
    all_to_all x1, waiting for transfers between devices, shards(): lax.all_to_all(jnp.stack(lax.psum(1, axis_name='expert') * [part], axis=0...  205 us
    ppermute x1, waiting for transfers between devices, shards(): summed = lax.ppermute(summed, ('dp', 'expert'), flip)  57.5 us
    ppermute x1, waiting for transfers between devices, shards(): part = lax.ppermute(part, ('dp', 'expert'), flip)  57.2 us
    all_to_all x4, waiting for transfers between devices, exchange(): block = lax.all_to_all(block, 'dp', split_axis=0, concat_axis=0, tiled=True)  39.8 us
    all_to_all x4, starting transfers between devices, exchange(): block = lax.all_to_all(block, 'dp', split_axis=0, concat_axis=0, tiled=True)  28.5 us
    unnamed x37, local copies, waits for them, and re-layouts  22 us
    unnamed x2, waiting for transfers between devices  18.8 us
    all_to_all x1, starting transfers between devices, shards(): lax.all_to_all(jnp.stack(lax.psum(1, axis_name='expert') * [part], axis=0...  18.8 us
  transfers between devices with their start and end apart: 8, of which 6 were waited for; matrix products, arithmetic and copies ran while one was open for 6% of the time, Pallas kernels for 0%

profile of v1, /device:TPU:14, one launch (start us, length us, event | category | flops | bytes accessed | tf_op | source)
XLA Modules:
  0.0 534.8 jit_solution(11185797284566019626)
XLA Ops:
  7.2 0.0 copy-start
  7.2 0.9 eq.24
  8.1 0.2 fusion.14
  8.3 0.8 broadcast_in_dim.31
  9.1 0.1 convert_element_type.48
  9.1 0.7 multiply_add_fusion.1
  9.8 0.2 iota_compare_fusion.1
  10.0 0.2 select_reduce_fusion
  10.2 3.2 multiply_convert_fusion
  13.4 7.3 %all-to-all-start.3 = ((bf16[16,32,2048]{2,1,0:T(8,128)(2,1)}), bf16[16,32,2048]{2,1,0:T(8,128)(2,1)}, u32[]{:S(2)}, u32[]{:S(2)}) async-start(bf16[16,32,2048]{2,1,0:T(8,128)(2,1)} %bitcast.69), calls=%async_computation.3 | async-start | bytes 4194304 | tf_op jit(solution)/shard_map/all_to_all | solution.py:81
  20.7 0.0 copy-done
  20.7 1.1 dynamic-slice_bitcast_fusion
  21.9 7.0 %collective-permute-start = (bf16[128,2304]{1,0:T(8,128)(2,1)S(1)}, bf16[128,2304]{1,0:T(8,128)(2,1)S(1)}, u32[]{:S(2)}, u32[]{:S(2)}) collective-permute-start(bf16[128,2304]{1,0:T(8,128)(2,1)S(1)} %pad_maximum_fusion.1), channel_id=1, source_target_pairs={{0,0},{1,16},{2,32},{3,48},{4,64},{5,80},{6,96},{7,112},{8,128},{9... | collective-permute-start | bytes 1769480 | tf_op jit(solution)/shard_map/ppermute | solution.py:55
  28.8 57.2 %collective-permute-done = bf16[128,2304]{1,0:T(8,128)(2,1)S(1)} collective-permute-done((bf16[128,2304]{1,0:T(8,128)(2,1)S(1)}, bf16[128,2304]{1,0:T(8,128)(2,1)S(1)}, u32[]{:S(2)}, u32[]{:S(2)}) %collective-permute-start) | collective-permute-done | bytes 589856 | tf_op jit(solution)/shard_map/ppermute | solution.py:55
  86.1 0.0 all-to-all-done.3
  86.1 4.5 stack.2
  90.6 18.8 %all-to-all-start.1 = ((bf16[16,128,2304]{2,1,0:T(8,128)(2,1)}), bf16[16,128,2304]{2,1,0:T(8,128)(2,1)}, u32[]{:S(2)}, u32[]{:S(2)}) async-start(bf16[16,128,2304]{2,1,0:T(8,128)(2,1)} %stack.2), calls=%async_computation.1 | async-start | bytes 18874368 | tf_op jit(solution)/shard_map/all_to_all | solution.py:57
  109.4 0.0 copy-done.7
  109.4 2.1 convolution_convert_fusion.3
  111.5 204.5 %all-to-all-done.1 = bf16[16,128,2304]{2,1,0:T(8,128)(2,1)} async-done(((bf16[16,128,2304]{2,1,0:T(8,128)(2,1)}), bf16[16,128,2304]{2,1,0:T(8,128)(2,1)}, u32[]{:S(2)}, u32[]{:S(2)}) %all-to-all-start.1) | async-done | bytes 9437216 | tf_op jit(solution)/shard_map/all_to_all | solution.py:57
  316.0 5.9 %all-to-all-start = ((bf16[16,32,2048]{2,1,0:T(8,128)(2,1)}), bf16[16,32,2048]{2,1,0:T(8,128)(2,1)S(1)}, u32[]{:S(2)}, u32[]{:S(2)}) async-start(bf16[16,32,2048]{2,1,0:T(8,128)(2,1)} %bitcast.5), calls=%async_computation | async-start | bytes 4194304 | tf_op jit(solution)/shard_map/all_to_all | solution.py:81
  321.9 0.2 reduce-scatter.4.cloned.1.call-start
  322.1 5.6 %fusion = f32[512,768]{1,0:T(8,128)} fusion(bf16[512,2048]{1,0:T(8,128)(2,1)} %bitcast.15, bf16[2048,2304]{1,0:T(8,128)(2,1)} %bitcast.10), kind=kOutput, calls=%fused_computation.8 | convolution fusion | flops 1610612736 | bytes 6815744 | tf_op jit(solution)/shard_map/dot_general | solution.py:91
  327.7 20.7 %all-to-all-done = bf16[16,32,2048]{2,1,0:T(8,128)(2,1)S(1)} async-done(((bf16[16,32,2048]{2,1,0:T(8,128)(2,1)}), bf16[16,32,2048]{2,1,0:T(8,128)(2,1)S(1)}, u32[]{:S(2)}, u32[]{:S(2)}) %all-to-all-start) | async-done | bytes 2097184 | tf_op jit(solution)/shard_map/all_to_all | solution.py:81
  348.5 4.5 fusion.5
  352.9 0.0 copy-done.5
  353.0 0.0 copy-done.13
  353.0 4.3 multiply_convert_fusion.2
  357.2 0.0 copy-start.14
  357.2 0.0 copy-start.11
  357.2 0.0 copy-start.9
  357.3 0.0 copy-start.6
  357.3 4.3 convolution_convert_fusion
  361.6 0.0 copy-done.14
  361.6 0.0 copy-done.11
  361.6 1.9 convolution_convert_fusion.1
  363.5 0.0 copy-done.9
  363.5 1.9 convolution_convert_fusion.2
  365.4 4.7 pad_maximum_fusion
  370.1 12.7 %copy.25 = bf16[2048,2304]{1,0:T(8,128)(2,1)} copy(bf16[2048,2304]{0,1:T(8,128)(2,1)} %pad_maximum_fusion) | data formatting | bytes 18874368
  382.7 0.0 reduce-scatter.4.cloned.1.call-update
  382.7 1.1 copy-done.12
  383.9 3.8 fusion.3
  387.7 5.1 add_convert_fusion
  392.8 7.4 %all-to-all-start.4 = ((bf16[16,32,2048]{2,1,0:T(8,128)(2,1)}), bf16[16,32,2048]{2,1,0:T(8,128)(2,1)S(1)}, u32[]{:S(2)}, u32[]{:S(2)}) async-start(bf16[16,32,2048]{2,1,0:T(8,128)(2,1)} %bitcast.75), calls=%async_computation.4 | async-start | bytes 4194304 | tf_op jit(solution)/shard_map/all_to_all | solution.py:81
  400.1 5.1 convolution_convert_fusion.4
  405.2 19.1 %all-to-all-done.4 = bf16[16,32,2048]{2,1,0:T(8,128)(2,1)S(1)} async-done(((bf16[16,32,2048]{2,1,0:T(8,128)(2,1)}), bf16[16,32,2048]{2,1,0:T(8,128)(2,1)S(1)}, u32[]{:S(2)}, u32[]{:S(2)}) %all-to-all-start.4) | async-done | bytes 2097184 | tf_op jit(solution)/shard_map/all_to_all | solution.py:81
  424.3 1.3 copy-done.3
  425.7 7.9 %all-to-all-start.2 = ((bf16[16,32,2048]{2,1,0:T(8,128)(2,1)}), bf16[16,32,2048]{2,1,0:T(8,128)(2,1)S(1)}, u32[]{:S(2)}, u32[]{:S(2)}) async-start(bf16[16,32,2048]{2,1,0:T(8,128)(2,1)} %bitcast.70), calls=%async_computation.2 | async-start | bytes 4194304 | tf_op jit(solution)/shard_map/all_to_all | solution.py:81
  433.6 2.3 fusion.15
  436.0 1.4 fusion.11
  437.3 18.8 %reduce-scatter.4.cloned.1.call-done = bf16[128,2304]{1,0:T(8,128)(2,1)} async-done(((bf16[2048,2304]{1,0:T(8,128)(2,1)}), bf16[128,2304]{1,0:T(8,128)(2,1)}) %reduce-scatter.4.cloned.1.call-update) | async-done | bytes 589840
  456.1 2.1 copy.26
  458.3 1.9 collective-permute-start.1
  460.2 0.0 all-to-all-done.2
  460.2 1.3 copy-done.2
  461.5 0.5 convolution_multiply_fusion
  462.0 0.0 copy-start.1
  462.0 3.2 fusion.12
  465.2 57.5 %collective-permute-done.1 = bf16[128,2304]{0,1:T(8,128)(2,1)} collective-permute-done((bf16[128,2304]{0,1:T(8,128)(2,1)}, bf16[128,2304]{0,1:T(8,128)(2,1)}, u32[]{:S(2)}, u32[]{:S(2)}) %collective-permute-start.1) | collective-permute-done | bytes 589856 | tf_op jit(solution)/shard_map/ppermute | solution.py:108
  522.7 1.8 slice_bitcast_fusion.2
  524.5 1.7 copy.22
  526.3 0.8 copy.23
  527.1 0.8 copy.24
  (21 shorter events, 0.1 us)
Async XLA Ops:
  7.2 13.5 %copy-start = (bf16[1,2048,768]{2,1,0:T(8,128)(2,1)S(1)}, bf16[1,2048,768]{2,1,0:T(8,128)(2,1)}, u32[]{:S(2)}) copy-start(bf16[1,2048,768]{2,1,0:T(8,128)(2,1)} %param.11) | copy-start | bytes 9437188
  13.4 72.7 %all-to-all-start.3 = ((bf16[16,32,2048]{2,1,0:T(8,128)(2,1)}), bf16[16,32,2048]{2,1,0:T(8,128)(2,1)}, u32[]{:S(2)}, u32[]{:S(2)}) async-start(bf16[16,32,2048]{2,1,0:T(8,128)(2,1)} %bitcast.69), calls=%async_computation.3 | async-start | bytes 4194304 | tf_op jit(solution)/shard_map/all_to_all | solution.py:81
  21.9 64.2 %collective-permute-start = (bf16[128,2304]{1,0:T(8,128)(2,1)S(1)}, bf16[128,2304]{1,0:T(8,128)(2,1)S(1)}, u32[]{:S(2)}, u32[]{:S(2)}) collective-permute-start(bf16[128,2304]{1,0:T(8,128)(2,1)S(1)} %pad_maximum_fusion.1), channel_id=1, source_target_pairs={{0,0},{1,16},{2,32},{3,48},{4,64},{5,80},{6,96},{7,112},{8,128},{9... | collective-permute-start | bytes 1769480 | tf_op jit(solution)/shard_map/ppermute | solution.py:55
  90.6 18.8 %copy-start.7 = (bf16[160,2048]{1,0:T(8,128)(2,1)S(1)}, bf16[160,2048]{1,0:T(8,128)(2,1)}, u32[]{:S(2)}) copy-start(bf16[160,2048]{1,0:T(8,128)(2,1)} %param.7) | copy-start | bytes 1966084
  90.6 225.4 %all-to-all-start.1 = ((bf16[16,128,2304]{2,1,0:T(8,128)(2,1)}), bf16[16,128,2304]{2,1,0:T(8,128)(2,1)}, u32[]{:S(2)}, u32[]{:S(2)}) async-start(bf16[16,128,2304]{2,1,0:T(8,128)(2,1)} %stack.2), calls=%async_computation.1 | async-start | bytes 18874368 | tf_op jit(solution)/shard_map/all_to_all | solution.py:57
  316.0 32.4 %all-to-all-start = ((bf16[16,32,2048]{2,1,0:T(8,128)(2,1)}), bf16[16,32,2048]{2,1,0:T(8,128)(2,1)S(1)}, u32[]{:S(2)}, u32[]{:S(2)}) async-start(bf16[16,32,2048]{2,1,0:T(8,128)(2,1)} %bitcast.5), calls=%async_computation | async-start | bytes 4194304 | tf_op jit(solution)/shard_map/all_to_all | solution.py:81
  321.9 134.2 %reduce-scatter.4.cloned.1.call-start = ((), (), s32[]{:S(2)}) async-start(), calls=%async_computation.6 | async-start | bytes 10027008
  348.5 4.5 copy-start.5
  348.5 4.5 copy-start.13
  357.2 4.4 copy-start.14
  357.2 4.4 copy-start.11
  357.2 6.3 %copy-start.9 = (bf16[512,768]{1,0:T(8,128)(2,1)}, bf16[512,768]{1,0:T(8,128)(2,1)S(1)}, u32[]{:S(2)}) copy-start(bf16[512,768]{1,0:T(8,128)(2,1)S(1)} %get-tuple-element.25) | copy-start | bytes 2359300
  357.3 4.3 copy-start.6
  382.7 1.1 copy-start.12
  383.8 3.8 copy-start.10
  392.8 7.4 %copy-start.15 = (bf16[512,768]{1,0:T(8,128)(2,1)S(1)}, bf16[512,768]{1,0:T(8,128)(2,1)}, u32[]{:S(2)}) copy-start(bf16[512,768]{1,0:T(8,128)(2,1)} %copy-done.14) | copy-start | bytes 2359300
  392.8 31.6 %all-to-all-start.4 = ((bf16[16,32,2048]{2,1,0:T(8,128)(2,1)}), bf16[16,32,2048]{2,1,0:T(8,128)(2,1)S(1)}, u32[]{:S(2)}, u32[]{:S(2)}) async-start(bf16[16,32,2048]{2,1,0:T(8,128)(2,1)} %bitcast.75), calls=%async_computation.4 | async-start | bytes 4194304 | tf_op jit(solution)/shard_map/all_to_all | solution.py:81
  424.3 1.3 copy-start.3
  424.3 9.3 %copy-start.8 = (f32[160,2]{0,1:T(2,128)S(1)}, f32[160,2]{0,1:T(2,128)}, u32[]{:S(2)}) copy-start(f32[160,2]{0,1:T(2,128)} %param.9) | copy-start | bytes 3844
  425.7 34.5 %all-to-all-start.2 = ((bf16[16,32,2048]{2,1,0:T(8,128)(2,1)}), bf16[16,32,2048]{2,1,0:T(8,128)(2,1)S(1)}, u32[]{:S(2)}, u32[]{:S(2)}) async-start(bf16[16,32,2048]{2,1,0:T(8,128)(2,1)} %bitcast.70), calls=%async_computation.2 | async-start | bytes 4194304 | tf_op jit(solution)/shard_map/all_to_all | solution.py:81
  433.6 2.3 copy-start.4
  458.3 64.4 %collective-permute-start.1 = (bf16[128,2304]{0,1:T(8,128)(2,1)}, bf16[128,2304]{0,1:T(8,128)(2,1)}, u32[]{:S(2)}, u32[]{:S(2)}) collective-permute-start(bf16[128,2304]{0,1:T(8,128)(2,1)} %copy.26), channel_id=1, source_target_pairs={{0,0},{1,16},{2,32},{3,48},{4,64},{5,80},{6,96},{7,112},{8,128},{9... | collective-permute-start | bytes 1769480 | tf_op jit(solution)/shard_map/ppermute | solution.py:108
  460.2 1.3 copy-start.2
  462.0 65.9 %copy-start.1 = (bf16[1,2048,768]{2,1,0:T(8,128)(2,1)S(1)}, bf16[1,2048,768]{2,1,0:T(8,128)(2,1)}, u32[]{:S(2)}) copy-start(bf16[1,2048,768]{2,1,0:T(8,128)(2,1)} %param.11) | copy-start | bytes 9437188
Sparse Core Ops, SparseCore 0:
  382.9 73.1 reduce-scatter.3
